TPU v7x, 32 devices: a whole 2x2x4 slice. The times are simulated.
32 devices in a mesh: kv: 4 (over y, x), tok: 8 (over z, core).
Axes of the slice: x: 2, y: 2, z: 4, core: 2. Of those that a mesh axis runs over, the one named last changes fastest.
Arguments:
- dec_tokens: bfloat16 [128, 5120], P('tok', 'kv'), may hold values from -60 to 60
- pre_tokens: bfloat16 [2048, 5120], P('tok', 'kv'), may hold values from -60 to 60
- w_query: bfloat16 [5120, 2560], P(None, 'kv'), may hold values from -0.078125 to 0.078125
- w_keyval: bfloat16 [5120, 2, 512], P(None, None, 'kv'), may hold values from -0.078125 to 0.078125
- b_query: float32 [2560], P('kv'), may hold values from -3 to 3
- b_keyval: float32 [2, 512], P(None, 'kv'), may hold values from -3 to 3
- dec_pool: bfloat16 [2, 98304, 512], P(None, 'tok', 'kv'), may hold values from -72 to 72
- owner_slots: int32 [128], P('tok'), may hold values from 0 to 127, each once
- dec_lengths: int32 [128], P('tok'), may hold values from 1 to 4096, as said below
- pre_cache: bfloat16 [2, 8192, 512], P(None, 'tok', 'kv'), may hold values from -72 to 72
- pre_offsets: int32 [4], replicated, may hold values from 1536 to 2048
Outputs:
- dec_attn: bfloat16 [128, 2560], P('tok', 'kv')
- pre_attn: bfloat16 [2048, 2560], P('tok', 'kv')
- new_pool: bfloat16 [2, 98304, 512], P(None, 'tok', 'kv')
- pre_keyval: bfloat16 [2, 2048, 512], P(None, 'tok', 'kv')
Inputs may be any that keep to these rules, and one draw needn't show every extreme that they name: `dec_lengths`: in the 16 slots of each owner, one length is 512 or more and the others are below 512, so an owner's lengths plus one each sum to at most 12288.
All inputs are finite; a program needn't handle non-finite values.
Results may differ from a plain program's by a relative error of at most 0.0065.
The roundings to bfloat16 on the way count: a program that leaves them out, or rounds other values in their place, can miss the bound.
Values may be sent and summed in bfloat16 or wider, within the bound.
A program may use at most 128 MiB of HBM per device.

v0:
```python
import jax
import jax.numpy as jnp
from jax import lax
from jax.sharding import PartitionSpec as P

HD = 128


THETA = 1000000.0


def swapped(value, axis, distance):
    return lax.ppermute(value, axis, [(i, i ^ 1 << distance) for i in range(lax.axis_size(axis))])


def rotate(values, positions):
    halfway = values.shape[-1] // 2
    spread = jnp.arange(halfway, dtype=jnp.float32) * (2.0 / values.shape[-1])
    rates = jnp.power(jnp.float32(THETA), -spread)
    angles = positions.astype(jnp.float32)[:, None] * rates[None, :]
    cosine = jnp.cos(angles)[:, None, :]
    sine = jnp.sin(angles)[:, None, :]
    former = values[..., :halfway]
    latter = values[..., halfway:]
    return jnp.concatenate(
        [former * cosine - latter * sine, latter * cosine + former * sine], axis=-1
    )


def head_scores(queries, key_rows, allowed):
    amount = queries.shape[0]
    q_heads = queries.shape[1] // HD
    shaped = queries.reshape(amount, q_heads, HD)
    product = jnp.einsum("ngd,md->ngm", shaped, key_rows, preferred_element_type=jnp.float32)
    scores = product * HD ** (-0.5)
    return jnp.where(allowed[:, None, :], scores, -jnp.inf)


def head_mix(scores, peaks, value_rows):
    powers = jnp.exp(scores - peaks[..., None])
    totals = jnp.sum(powers, axis=-1)
    weights = powers.astype(jnp.bfloat16)
    product = jnp.einsum("ngm,md->ngd", weights, value_rows, preferred_element_type=jnp.float32)
    return (totals, product)


def serve_owner(queries, keyval, lengths, cache_pool):
    amount = queries.shape[0]
    q_heads = queries.shape[1] // HD
    kv_heads = cache_pool.shape[2] // HD
    finish = jnp.cumsum(lengths + 1)
    starts = finish - lengths - 1
    turned = rotate(queries.astype(jnp.float32).reshape(amount, q_heads, HD), lengths)
    turned = turned.astype(jnp.bfloat16).reshape(amount, q_heads * HD)
    new_keys = rotate(keyval[:, 0].astype(jnp.float32).reshape(amount, kv_heads, HD), lengths)
    new_keys = new_keys.astype(jnp.bfloat16).reshape(amount, kv_heads * HD)
    appended = jnp.stack([new_keys, keyval[:, 1]], axis=0)
    cache_pool = cache_pool.at[:, starts + lengths].set(appended)
    spots = jnp.arange(cache_pool.shape[1], dtype=jnp.int32)
    allowed = (spots[None, :] >= starts[:, None]) & (spots[None, :] <= (starts + lengths)[:, None])
    scores = head_scores(turned, cache_pool[0], allowed)
    totals, mixed = head_mix(scores, jnp.max(scores, axis=-1), cache_pool[1])
    result = (mixed / totals[..., None]).astype(jnp.bfloat16).reshape(amount, q_heads * HD)
    return (result, cache_pool)


def body(
    dec_tokens,
    pre_tokens,
    w_query,
    w_keyval,
    b_query,
    b_keyval,
    dec_pool,
    owner_slots,
    dec_lengths,
    pre_cache,
    pre_offsets,
):
    dec_count = dec_tokens.shape[0]
    pre_count = pre_tokens.shape[0]
    q_width = w_query.shape[1]
    kv_width = w_keyval.shape[2]
    kv_weight = w_keyval.reshape(w_keyval.shape[0], 2 * kv_width)
    stacked = jnp.concatenate([dec_tokens, pre_tokens], axis=0)
    columns = lax.all_gather(stacked, "kv", axis=1, tiled=True)
    all_query = jnp.dot(columns, w_query, preferred_element_type=jnp.float32)
    all_keyval = jnp.dot(columns, kv_weight, preferred_element_type=jnp.float32)
    all_query = all_query + b_query
    all_keyval = all_keyval + b_keyval.reshape(2 * kv_width)
    dec_query = all_query[:dec_count].astype(jnp.bfloat16)
    dec_keyval = all_keyval[:dec_count].astype(jnp.bfloat16).reshape(dec_count, 2, kv_width)
    every_query, every_keyval = (
        lax.all_gather(dec_query, "tok", axis=0, tiled=True),
        lax.all_gather(dec_keyval, "tok", axis=0, tiled=True),
    )
    served, new_pool = serve_owner(
        jnp.take(every_query, owner_slots, axis=0),
        jnp.take(every_keyval, owner_slots, axis=0),
        dec_lengths,
        dec_pool,
    )
    every_result = lax.all_gather(served, "tok", axis=0, tiled=True)
    every_owner = lax.all_gather(owner_slots, "tok", axis=0, tiled=True)
    inverse = (
        jnp.zeros(every_owner.shape, jnp.int32)
        .at[every_owner]
        .set(jnp.arange(every_owner.shape[0], dtype=jnp.int32))
    )
    wanted = lax.axis_index("tok") * dec_count + jnp.arange(dec_count, dtype=jnp.int32)
    dec_attn = jnp.take(every_result, jnp.take(inverse, wanted), axis=0)
    tok_place = lax.axis_index("tok")
    half_id = tok_place % 2
    offset = pre_offsets[tok_place // 2]
    local_pos = jnp.arange(pre_count, dtype=jnp.int32)
    positions = offset + half_id * pre_count + local_pos
    q_heads = q_width // HD
    kv_heads = kv_width // HD
    turned = rotate(all_query[dec_count:].reshape(pre_count, q_heads, HD), positions)
    turned = turned.astype(jnp.bfloat16).reshape(pre_count, q_width)
    pre_kv = all_keyval[dec_count:].reshape(pre_count, 2, kv_width)
    new_keys = rotate(pre_kv[:, 0].reshape(pre_count, kv_heads, HD), positions)
    new_keys = new_keys.astype(jnp.bfloat16).reshape(pre_count, kv_width)
    appended = jnp.stack([new_keys, pre_kv[:, 1].astype(jnp.bfloat16)], axis=0)
    shard = pre_cache.shape[1]
    other_cache, other_new = swapped((pre_cache, appended), "tok", 0)
    is_lower = half_id == 0
    history = jnp.where(
        is_lower,
        jnp.concatenate([pre_cache, other_cache], axis=1),
        jnp.concatenate([other_cache, pre_cache], axis=1),
    )
    block_rows = jnp.where(
        is_lower,
        jnp.concatenate([appended, other_new], axis=1),
        jnp.concatenate([other_new, appended], axis=1),
    )
    key_rows = jnp.concatenate([history, block_rows], axis=1)
    key_slots = jnp.arange(key_rows.shape[1], dtype=jnp.int32)
    key_pos = jnp.where(key_slots < 2 * shard, key_slots, offset + key_slots - 2 * shard)
    usable = (key_slots < offset) | (key_slots >= 2 * shard)
    allowed = usable[None, :] & (key_pos[None, :] <= positions[:, None])
    scores = head_scores(turned, key_rows[0], allowed)
    totals, mixed = head_mix(scores, jnp.max(scores, axis=-1), key_rows[1])
    pre_attn = (mixed / totals[..., None]).astype(jnp.bfloat16).reshape(pre_count, q_width)
    return (dec_attn, pre_attn, new_pool, appended)


def solution(mesh):
    in_specs = (
        P("tok", "kv"),
        P("tok", "kv"),
        P(None, "kv"),
        P(None, None, "kv"),
        P("kv"),
        P(None, "kv"),
        P(None, "tok", "kv"),
        P("tok"),
        P("tok"),
        P(None, "tok", "kv"),
        P(),
    )
    out_specs = (P("tok", "kv"), P("tok", "kv"), P(None, "tok", "kv"), P(None, "tok", "kv"))
    return jax.shard_map(body, mesh=mesh, in_specs=in_specs, out_specs=out_specs, check_vma=False)
```

profile of v0, /device:TPU:0, one launch (start us, length us, event | category | flops | bytes accessed | tf_op | source)
XLA Modules:
  0.0 155.6 jit_solution(4906346320083716606)
XLA Ops:
  7.3 6.5 %copy.145 = bf16[2,12288,128]{2,1,0:T(8,128)(2,1)} copy(bf16[2,12288,128]{2,1,0:T(8,128)(2,1)} %param.19) | data formatting | bytes 12582912
  13.8 0.9 pad_maximum_fusion
  19.7 10.2 %all-reduce = s32[128]{0:T(128)S(1)} all-reduce(s32[128]{0:T(128)S(1)} %dynamic-update-slice), channel_id=1, replica_groups=mesh['kv'=4,'tok'=8] {'tok'}, use_global_device_ids=true, to_apply=%add | all-reduce | flops 128 | bytes 1024
  29.9 1.0 scatter_custom_fusion.1
  31.7 1.2 multiply_cosine_fusion.1
  33.7 1.2 maximum_select_fusion
  34.9 23.7 %all-gather.2.cloned.1.call-done = bf16[272,5120]{1,0:T(8,128)(2,1)} async-done(((bf16[272,1280]{1,0:T(8,128)(2,1)}), bf16[272,5120]{1,0:T(8,128)(2,1)}) %all-gather.2.cloned.1.call-update) | async-done | bytes 2785296 | tf_op jit(solution)/shard_map/all_gather | solution.py:86
  58.6 3.5 %fusion.15 = f32[272,256]{1,0:T(8,128)S(1)} fusion(bf16[272,5120]{1,0:T(8,128)(2,1)} %all-gather.2.cloned.1.call-done, bf16[640,8,2,128]{3,2,1,0:T(2,128)(2,1)} %bitcast.74, f32[256]{0:T(256)S(1)} %bitcast.75), kind=kOutput, calls=%fused_computation.29 | convolution fusion | flops 713101312 | bytes 5686272 | tf_op jit(solution)/shard_map/dot_general | solution.py:88
  62.8 6.1 %convolution_add_fusion = f32[272,640]{1,0:T(8,128)S(1)} fusion(bf16[272,5120]{1,0:T(8,128)(2,1)} %all-gather.2.cloned.1.call-done, bf16[5120,640]{1,0:T(8,128)(2,1)} %param.15, f32[640]{0:T(1024)S(1)} %copy-done.5), kind=kOutput, calls=%fused_computation.28 | convolution fusion | flops 1782753280 | bytes 10037760 | tf_op jit(solution)/shard_map/dot_general | solution.py:87
  69.5 0.8 pad_maximum_fusion.2
  71.0 14.0 %all_gather.17 = bf16[128,2,128]{2,1,0:T(2,128)(2,1)S(1)} all-gather(bf16[16,2,128]{2,1,0:T(2,128)(2,1)S(1)} %reshape.475), channel_id=1, replica_groups=mesh['kv'=4,'tok'=8] {'tok'}, dimensions={0}, use_global_device_ids=true | all-gather | bytes 73728 | tf_op jit(solution)/shard_map/all_gather | solution.py:95
  85.8 14.2 %all_gather.16 = bf16[128,640]{1,0:T(8,128)(2,1)S(1)} all-gather(bf16[16,640]{1,0:T(8,128)(2,1)S(1)} %slice.145), channel_id=1, replica_groups=mesh['kv'=4,'tok'=8] {'tok'}, dimensions={0}, use_global_device_ids=true | all-gather | bytes 184320 | tf_op jit(solution)/shard_map/all_gather | solution.py:94
  100.9 2.3 %scatter_fusion = bf16[2,12288,128]{2,1,0:T(8,128)(2,1)} fusion(bf16[2,12288,128]{2,1,0:T(8,128)(2,1)} %copy.145, s32[16]{0:T(128)S(1)} %get-tuple-element.35, bf16[16,2,128]{2,0,1:T(8,128)(2,1)S(1)} %maximum_bitcast_fusion), kind=kCustom, calls=%fused_computation.4 | custom fusion | bytes 24640 | tf_op jit(solution)/shard_map/scatter | solution.py:58
  103.3 3.4 %fusion.84 = (f32[16,5]{0,1:T(8,128)S(1)}, f32[16,5,12288]{2,0,1:T(8,128)S(1)}) fusion(bf16[2,12288,128]{2,1,0:T(8,128)(2,1)} %scatter_fusion, bf16[16,5,64]{2,0,1:T(8,128)(2,1)S(1)} %get-tuple-element.46, bf16[16,5,64]{2,0,1:T(8,128)(2,1)S(1)} %get-tuple-element.45, pred[16,12288]{1,0:T(8,128)(4,1)S(1)} %fusion.33), kind=kOutput, calls=%fused_computation.132 | convolution fusion | flops 254648240 | bytes 7295296 | tf_op jit(solution)/shard_map/ngd,md->ngm/dot_general | solution.py:34
  106.7 0.8 fusion.7
  107.5 0.9 fusion.24
  108.3 14.0 %all_gather.18 = bf16[128,640]{1,0:T(8,128)(2,1)S(1)} all-gather(bf16[16,640]{1,0:T(8,128)(2,1)S(1)} %bitcast.73), channel_id=1, replica_groups=mesh['kv'=4,'tok'=8] {'tok'}, dimensions={0}, use_global_device_ids=true | all-gather | bytes 184320 | tf_op jit(solution)/shard_map/all_gather | solution.py:103
  123.0 1.1 subtract_convert_fusion
  124.1 0.7 broadcast_select_fusion
  124.8 1.1 maximum_select_fusion.1
  125.9 6.6 %fusion.1 = (f32[256,5]{0,1:T(8,128)S(1)}, f32[256,5,2560]{2,0,1:T(8,128)}) fusion(pred[256,2560]{1,0:T(8,128)(4,1)S(1)} %compare_and_fusion, bf16[2,2048,128]{2,1,0:T(8,128)(2,1)S(1)} %copy-done, bf16[2,512,128]{2,1,0:T(8,128)(2,1)S(1)} %maximum_select_fusion.1, bf16[256,5,64]{2,0,1:T(8,128)(2,1)S(1)} %get-tuple-element.38, ...), kind=kOutput, calls=%fused_computation.10 | convolution fusion | flops 850656000 | bytes 15406080 | tf_op jit(solution)/shard_map/ngd,md->ngm/dot_general | solution.py:34
  132.5 8.4 %fusion.2 = f32[256,5]{0,1:T(8,128)S(1)} fusion(f32[256,5,2560]{2,0,1:T(8,128)} %get-tuple-element.63, f32[256,5]{0,1:T(8,128)S(1)} %get-tuple-element.62, pred[256,2560]{1,0:T(8,128)(4,1)S(1)} %compare_and_fusion), kind=kLoop, calls=%fused_computation.11 | loop fusion | flops 13105920 | bytes 13772800 | tf_op jit(solution)/shard_map/reduce_sum | solution.py:41
  140.9 7.0 %fusion.30 = bf16[256,5,128]{0,2,1:T(8,128)(2,1)S(1)} fusion(f32[256,5,2560]{2,0,1:T(8,128)} %get-tuple-element.63, f32[256,5]{0,1:T(8,128)S(1)} %get-tuple-element.62, pred[256,2560]{1,0:T(8,128)(4,1)S(1)} %compare_and_fusion, bf16[2,512,128]{2,1,0:T(8,128)(2,1)S(1)} %maximum_select_fusion.1, bf16[2,2048,128]{2,1,0:T(8,128)(2,1)S(1)} %copy-done, ...), kind=kOutput, calls=%fused_computation.35 | convolution fusion | flops 853606400 | bytes 15411200 | tf_op jit(solution)/shard_map/ngm,md->ngd/dot_general | solution.py:43
  147.9 0.9 copy.100
  (84 shorter events, 9.4 us)
Async XLA Ops:
  7.2 11.0 %copy-start.9 = (u32[32]{0:T(128)S(1)}, u32[32]{0:T(128)}, u32[]{:S(2)}) copy-start(u32[32]{0:T(128)} %constant.100) | copy-start | bytes 388
  7.2 6.6 %copy-start.3 = (bf16[16,1280]{1,0:T(8,128)(2,1)S(1)}, bf16[16,1280]{1,0:T(8,128)(2,1)}, u32[]{:S(2)}) copy-start(bf16[16,1280]{1,0:T(8,128)(2,1)} %param.13) | copy-start | bytes 122884
  7.2 6.6 %copy-start.1 = (bf16[256,1280]{1,0:T(8,128)(2,1)S(1)}, bf16[256,1280]{1,0:T(8,128)(2,1)}, u32[]{:S(2)}) copy-start(bf16[256,1280]{1,0:T(8,128)(2,1)} %param.14) | copy-start | bytes 1966084
  7.2 10.6 %copy-start.8 = (s32[16]{0:T(128)S(1)}, s32[16]{0:T(128)}, u32[]{:S(2)}) copy-start(s32[16]{0:T(128)} %param.20) | copy-start | bytes 196
  7.2 10.7 %copy-start.4 = (s32[16]{0:T(128)S(1)}, s32[16]{0:T(128)}, u32[]{:S(2)}) copy-start(s32[16]{0:T(128)} %param.21) | copy-start | bytes 196
  7.2 7.5 %copy-start.2 = (bf16[2,1024,128]{2,1,0:T(8,128)(2,1)S(1)}, bf16[2,1024,128]{2,1,0:T(8,128)(2,1)}, u32[]{:S(2)}) copy-start(bf16[2,1024,128]{2,1,0:T(8,128)(2,1)} %param.22) | copy-start | bytes 1572868
  7.2 8.0 %copy-start.7 = (s32[4]{0:T(128)S(1)}, s32[4]{0:T(128)}, u32[]{:S(2)}) copy-start(s32[4]{0:T(128)} %param.23) | copy-start | bytes 52
  7.2 51.3 %all-gather.2.cloned.1.call-start = ((), (), s32[]{:S(2)}) async-start(), calls=%async_computation | async-start | bytes 3481600 | tf_op jit(solution)/shard_map/all_gather | solution.py:86
  13.8 44.8 %copy-start.6 = (f32[2,128]{1,0:T(2,128)S(1)}, f32[2,128]{1,0:T(2,128)}, u32[]{:S(2)}) copy-start(f32[2,128]{1,0:T(2,128)} %param.18) | copy-start | bytes 3076
  14.7 18.9 %collective-permute-start = (bf16[2,1024,128]{2,1,0:T(8,128)(2,1)S(1)}, bf16[2,1024,128]{2,1,0:T(8,128)(2,1)S(1)}, u32[]{:S(2)}, u32[]{:S(2)}) collective-permute-start(bf16[2,1024,128]{2,1,0:T(8,128)(2,1)S(1)} %copy-done.2), channel_id=1, source_target_pairs={{0,1},{1,0},{2,3},{3,2},{4,5},{5,4},{6,7},{7,6},{8,9},{9,8},{10,11... | collective-permute-start | bytes 1572872 | tf_op jit(solution)/shard_map/ppermute | solution.py:13
  58.6 4.2 %copy-start.5 = (f32[640]{0:T(1024)S(1)}, f32[640]{0:T(1024)}, u32[]{:S(2)}) copy-start(f32[640]{0:T(1024)} %param.17) | copy-start | bytes 7684
  70.2 54.5 %collective-permute-start.1 = (bf16[2,256,128]{2,1,0:T(8,128)(2,1)}, bf16[2,256,128]{2,1,0:T(8,128)(2,1)}, u32[]{:S(2)}, u32[]{:S(2)}) collective-permute-start(bf16[2,256,128]{2,1,0:T(8,128)(2,1)} %pad_maximum_fusion.2), channel_id=1, source_target_pairs={{0,1},{1,0},{2,3},{3,2},{4,5},{5,4},{6,7},{7,6},{8,9},{9,8},{10,11... | collective-permute-start | bytes 393224 | tf_op jit(solution)/shard_map/ppermute | solution.py:13
  103.2 4.2 %slice-start = ((s8[6291456]{0:T(1024)(128)(4,1)}), s8[4194304]{0:T(1024)(128)(4,1)S(1)}, s32[]{:S(2)}) async-start(s8[6291456]{0:T(1024)(128)(4,1)} %bitcast.67), calls=%async_computation.1 | async-start | bytes 8388608
  103.3 4.2 %slice-start.1 = ((s8[6291456]{0:T(1024)(128)(4,1)}), s8[2097152]{0:T(1024)(128)(4,1)S(1)}, s32[]{:S(2)}) async-start(s8[6291456]{0:T(1024)(128)(4,1)} %bitcast.67), calls=%async_computation.2 | async-start | bytes 4194304
  107.5 18.4 %copy-start = (bf16[2,2048,128]{2,1,0:T(8,128)(2,1)S(1)}, bf16[2,2048,128]{2,1,0:T(8,128)(2,1)}, u32[]{:S(2)}) copy-start(bf16[2,2048,128]{2,1,0:T(8,128)(2,1)} %maximum_select_fusion) | copy-start | bytes 3145732
Sparse Core Ops, SparseCore 0:
  14.8 43.6 all-gather.1
where the time goes:
time: 156 us
  blocking collectives  52.5 us (34%)
  matrix products  27.4 us (18%)
  waiting for transfers between devices  23.7 us (15%)
  other arithmetic  19.5 us (12%)
  local copies, waits for them, and re-layouts  16.2 us (10%)
  between operations  15.8 us (10%)
    all_gather x1, waiting for transfers between devices, body(): columns = lax.all_gather(stacked, 'kv', axis=1, tiled=True)  23.7 us
    all_gather x1, blocking collectives, body(): lax.all_gather(dec_query, 'tok', axis=0, tiled=True)  14.2 us
    all_gather x1, blocking collectives, body(): every_result = lax.all_gather(served, 'tok', axis=0, tiled=True)  14 us
    all_gather x1, blocking collectives, body(): lax.all_gather(dec_keyval, 'tok', axis=0, tiled=True)  14 us
    unnamed x1, blocking collectives  10.2 us
    dot_general x2, matrix products, head_scores(): jnp.einsum('ngd,md->ngm', shaped, key_rows, preferred_element_type=jnp.fl...  10 us
    reduce_sum x2, other arithmetic, head_mix(): totals = jnp.sum(powers, axis=-1)  9.2 us
    unnamed x31, local copies, waits for them, and re-layouts  8.76 us
  transfers between devices with their start and end apart: 3, of which 1 were waited for; matrix products, arithmetic and copies ran while one was open for 13% of the time, Pallas kernels for 0%

commit v1 on v0

v1 whole, which is shorter than its diff:
```python
import functools

import jax
import jax.numpy as jnp
import numpy as np
from jax import lax
from jax.experimental import pallas as pl
from jax.experimental.pallas import tpu as pltpu
from jax.sharding import PartitionSpec as P

HD = 128
THETA = 1000000.0
MESH = pl.DeviceIdType.MESH
CHUNKS = 4
F32 = jnp.float32
BF16 = jnp.bfloat16


def rotated(value, cosine, sine):
    return value * cosine + pltpu.roll(value, HD // 2, 1) * sine


def dot_nt(a, b):
    return lax.dot_general(a, b, (((1,), (1,)), ((), ())), preferred_element_type=F32)


def step_kernel(
    n_tok,
    dec_x, pre_x, w_q, w_kv, b_q, b_kv, pool, slots, lengths, cache, offsets, rates,
    o_dec, o_pre, o_kv, o_new,
    xd, xp, w, raw, kvpool, hist, nk, qs, ms, ls, acc, dq_own, dq_all, dr_send, dr_recv,
    l_sem, ds_sem, dr_sem, ps_sem, pr_sem, qs_sem, qr_sem, rs_sem, rr_sem,
    cs_sem, cr_sem, ks_sem, kr_sem,
):
    kv = lax.axis_index("kv")
    tok = lax.axis_index("tok")
    mate = tok + 1 - 2 * lax.rem(tok, 2)
    half = lax.rem(tok, 2)
    px = kv + 1 - 2 * lax.rem(kv, 2)
    py = lax.rem(kv + 2, 4)
    pd = lax.rem(px + 2, 4)
    dec_rows, width = dec_x.shape
    pre_rows = pre_x.shape[0]
    q_width = w_q.shape[1]
    heads = q_width // HD
    rows = pre_rows // CHUNKS
    mid = rows // 2
    shard = cache.shape[1]
    scale = HD ** -0.5

    loads = [
        pltpu.make_async_copy(w_kv, raw, l_sem.at[0]),
        pltpu.make_async_copy(w_q, w.at[:, pl.ds(0, q_width)], l_sem.at[1]),
        pltpu.make_async_copy(dec_x, xd.at[kv], l_sem.at[2]),
        pltpu.make_async_copy(pre_x, xp.at[kv], l_sem.at[3]),
        pltpu.make_async_copy(
            cache, hist.at[:, pl.ds(pl.multiple_of(half * shard, shard), shard)], l_sem.at[4]
        ),
        pltpu.make_async_copy(pool, kvpool, l_sem.at[5]),
    ]
    for load in loads:
        load.start()

    barrier = pltpu.get_barrier_semaphore()
    for peer in (px, py, pd):
        pl.semaphore_signal(barrier, inc=1, device_id=(peer, tok), device_id_type=MESH)
    for d in range(1, n_tok):
        pl.semaphore_signal(
            barrier, inc=1, device_id=(kv, lax.rem(tok + d, n_tok)), device_id_type=MESH
        )
    pl.semaphore_wait(barrier, n_tok + 2)

    def remote(src, dst, send, recv, where):
        return pltpu.make_async_remote_copy(
            src_ref=src, dst_ref=dst, send_sem=send, recv_sem=recv,
            device_id=where, device_id_type=MESH,
        )

    dec_sends = [
        remote(dec_x, xd.at[kv], ds_sem.at[i], dr_sem.at[i], (peer, tok))
        for i, peer in enumerate((px, py, pd))
    ]
    for send in dec_sends:
        send.start()

    def own_sends(r):
        part = pl.ds(r * rows, rows)
        return [
            remote(pre_x.at[part], xp.at[kv, part], ps_sem.at[r, i], pr_sem.at[r, i], (peer, tok))
            for i, peer in enumerate((px, py))
        ]

    def forwards(r):
        first, second = pl.ds(r * rows, mid), pl.ds(r * rows + mid, mid)
        return [
            remote(xp.at[py, first], xp.at[py, first], ps_sem.at[r, 2], pr_sem.at[r, 2], (px, tok)),
            remote(xp.at[px, second], xp.at[px, second], ps_sem.at[r, 3], pr_sem.at[r, 3], (py, tok)),
        ]

    own = [own_sends(r) for r in range(CHUNKS)]
    onward = [forwards(r) for r in range(CHUNKS)]
    for r in range(2):
        for send in own[r]:
            send.start()
    hist_part = hist.at[:, pl.ds(pl.multiple_of(half * shard, shard), shard)]
    cache_send = remote(cache, hist_part, cs_sem, cr_sem, (kv, mate))
    cache_send.start()

    def pump(r):
        for send in own[r]:
            send.wait_recv()
        for send in onward[r]:
            send.start()
        if r + 2 < CHUNKS:
            for send in own[r + 2]:
                send.start()

    loads[0].wait()
    block = 512
    row = lax.broadcasted_iota(jnp.int32, (block, block), 0)
    col = lax.broadcasted_iota(jnp.int32, (block, block), 1)
    wanted = jnp.where(row < block // 2, 2 * row, 2 * row - block + 1)
    permute = jnp.where(col == wanted, 1.0, 0.0).astype(BF16)

    def part_weights(i, carry):
        tile = raw[pl.ds(pl.multiple_of(i * block, block), block), :]
        parted = jnp.dot(permute, tile, preferred_element_type=F32).astype(BF16)
        where = pl.ds(pl.multiple_of(i * (block // 2), block // 2), block // 2)
        w[where, pl.ds(q_width, HD)] = parted[: block // 2]
        w[where, pl.ds(q_width + HD, HD)] = parted[block // 2:]
        return carry

    lax.fori_loop(0, raw.shape[0] // block, part_weights, 0)

    def project(x_ref, start, amount):
        def add(s, total):
            return total + jnp.dot(
                x_ref[s, pl.ds(start, amount), :],
                w[pl.ds(pl.multiple_of(s * width, width), width), :],
                preferred_element_type=F32,
            )

        total = lax.fori_loop(0, 4, add, jnp.zeros((amount, q_width + 2 * HD), F32))
        bias = jnp.concatenate([b_q[...], b_kv[0:1, :], b_kv[1:2, :]], axis=1)
        return total + bias

    loads[1].wait()
    loads[2].wait()
    for send in dec_sends:
        send.wait_recv()
    dq_own[...] = project(xd, 0, dec_rows).astype(BF16)
    q_sends = [
        remote(dq_own, dq_all.at[tok], qs_sem.at[d - 1], qr_sem.at[d - 1],
               (kv, lax.rem(tok + d, n_tok)))
        for d in range(1, n_tok)
    ]
    for send in q_sends:
        send.start()
    dq_all[tok] = dq_own[...]

    pump(0)
    pump(1)

    for send in q_sends:
        send.wait_recv()
    requests = n_tok * dec_rows
    row = lax.broadcasted_iota(jnp.int32, (dec_rows, requests), 0)
    col = lax.broadcasted_iota(jnp.int32, (dec_rows, requests), 1)
    row_t = lax.broadcasted_iota(jnp.int32, (requests, dec_rows), 0)
    col_t = lax.broadcasted_iota(jnp.int32, (requests, dec_rows), 1)
    stacked = heads * dec_rows
    slot_of = lax.rem(lax.broadcasted_iota(jnp.int32, (stacked, 1), 0), dec_rows)
    line = lax.broadcasted_iota(jnp.int32, (dec_rows, HD), 0)
    chosen = jnp.zeros((dec_rows, requests), F32)
    chosen_t = jnp.zeros((requests, dec_rows), F32)
    first = jnp.zeros((stacked, 1), jnp.int32)
    last = jnp.zeros((stacked, 1), jnp.int32)
    places = jnp.zeros((dec_rows, HD), jnp.int32)
    begin = jnp.int32(0)
    for s in range(dec_rows):
        request = slots[s]
        length = lengths[s]
        chosen = jnp.where((row == s) & (col == request), 1.0, chosen)
        chosen_t = jnp.where((col_t == s) & (row_t == request), 1.0, chosen_t)
        first = jnp.where(slot_of == s, begin, first)
        last = jnp.where(slot_of == s, begin + length, last)
        places = jnp.where(line == s, length, places)
        begin = begin + length + 1
    chosen = chosen.astype(BF16)
    chosen_t = chosen_t.astype(BF16)
    every = dq_all[...].reshape(requests, q_width + 2 * HD)
    mine = jnp.dot(chosen, every, preferred_element_type=F32)
    lane = lax.broadcasted_iota(jnp.int32, (1, HD), 1)
    sign = jnp.where(lane < HD // 2, -1.0, 1.0)
    angles = places.astype(F32) * rates[...]
    cosine = jnp.cos(angles)
    sine = jnp.sin(angles) * sign
    turned = jnp.concatenate(
        [rotated(mine[:, h * HD:(h + 1) * HD], cosine, sine) for h in range(heads)], axis=0
    ).astype(BF16)
    fresh_k = rotated(mine[:, q_width:q_width + HD], cosine, sine).astype(BF16)
    fresh_v = mine[:, q_width + HD:].astype(BF16)
    o_new[0] = fresh_k
    o_new[1] = fresh_v
    same = slot_of == lax.broadcasted_iota(jnp.int32, (stacked, dec_rows), 1)
    scores = jnp.where(same, dot_nt(turned, fresh_k) * scale, -jnp.inf)
    peak = jnp.max(scores, axis=1, keepdims=True)
    powers = jnp.exp(scores - peak)
    total = jnp.sum(powers, axis=1, keepdims=True)
    mixed = jnp.dot(powers.astype(BF16), fresh_v, preferred_element_type=F32)
    loads[5].wait()
    tile = 2048

    def visit(t, carry):
        peak, total, mixed = carry
        where = pl.ds(pl.multiple_of(t * tile, tile), tile)
        spots = t * tile + lax.broadcasted_iota(jnp.int32, (stacked, tile), 1)
        scores = dot_nt(turned, kvpool[0, where, :]) * scale
        scores = jnp.where((spots >= first) & (spots < last), scores, -jnp.inf)
        top = jnp.maximum(peak, jnp.max(scores, axis=1, keepdims=True))
        powers = jnp.exp(scores - top)
        fade = jnp.exp(peak - top)
        total = total * fade + jnp.sum(powers, axis=1, keepdims=True)
        mixed = mixed * fade + jnp.dot(
            powers.astype(BF16), kvpool[1, where, :], preferred_element_type=F32
        )
        return top, total, mixed

    peak, total, mixed = lax.fori_loop(0, pool.shape[1] // tile, visit, (peak, total, mixed))
    result = (mixed / total).astype(BF16)
    result = jnp.concatenate(
        [result[h * dec_rows:(h + 1) * dec_rows] for h in range(heads)], axis=1
    )
    spread = jnp.dot(chosen_t, result, preferred_element_type=F32).astype(BF16)
    dr_send[...] = spread.reshape(n_tok, dec_rows, q_width)
    r_sends = []
    for d in range(1, n_tok):
        peer = lax.rem(tok + d, n_tok)
        r_sends.append(
            remote(dr_send.at[peer], dr_recv.at[tok], rs_sem.at[d - 1], rr_sem.at[d - 1],
                   (kv, peer))
        )
    for send in r_sends:
        send.start()
    dr_recv[tok] = dr_send[tok]
    pump(2)

    offset = offsets[lax.div(tok, 2)]
    loads[3].wait()
    loads[4].wait()
    cache_send.wait_recv()
    key_sends = []
    for r in range(CHUNKS):
        for send in onward[r]:
            send.wait_recv()
        value = project(xp, r * rows, rows)
        place = pl.multiple_of(half * pre_rows + r * rows, rows)
        positions = offset + place + lax.broadcasted_iota(jnp.int32, (rows, HD), 0)
        angles = positions.astype(F32) * rates[...]
        cosine = jnp.cos(angles)
        sine = jnp.sin(angles) * sign
        queries = jnp.concatenate(
            [rotated(value[:, h * HD:(h + 1) * HD], cosine, sine) for h in range(heads)], axis=0
        ).astype(BF16)
        qs[r] = queries
        new_k = rotated(value[:, q_width:q_width + HD], cosine, sine).astype(BF16)
        new_v = value[:, q_width + HD:].astype(BF16)
        o_kv[0, pl.ds(r * rows, rows), :] = new_k
        o_kv[1, pl.ds(r * rows, rows), :] = new_v
        nk[0, pl.ds(place, rows), :] = new_k
        nk[1, pl.ds(place, rows), :] = new_v
        part = nk.at[:, pl.ds(place, rows)]
        send = remote(part, part, ks_sem.at[r], kr_sem.at[r], (kv, mate))
        send.start()
        key_sends.append(send)
        if r == 0:
            pump(3)
        scores = dot_nt(queries, hist[0]) * scale
        cached = lax.broadcasted_iota(jnp.int32, (1, 2 * shard), 1) < offset
        scores = jnp.where(cached, scores, -jnp.inf)
        peak = jnp.max(scores, axis=1, keepdims=True)
        powers = jnp.exp(scores - peak)
        total = jnp.sum(powers, axis=1, keepdims=True)
        acc[r] = jnp.dot(powers.astype(BF16), hist[1], preferred_element_type=F32)
        ms[r] = jnp.broadcast_to(peak, (heads * rows, HD))
        ls[r] = jnp.broadcast_to(total, (heads * rows, HD))

    for send in r_sends:
        send.wait_recv()
    gathered = dr_recv[0].astype(F32)
    for o in range(1, n_tok):
        gathered = gathered + dr_recv[o].astype(F32)
    o_dec[...] = gathered.astype(BF16)

    for send in key_sends:
        send.wait_recv()
    inner = lax.rem(lax.broadcasted_iota(jnp.int32, (heads * rows, 1), 0), rows)
    later = lax.broadcasted_iota(jnp.int32, (heads * rows, 2 * pre_rows), 1)

    def finish(r, carry):
        scores = dot_nt(qs[r], nk[0]) * scale
        scores = jnp.where(later <= inner + (half * pre_rows + r * rows), scores, -jnp.inf)
        peak = ms[r][:, :1]
        top = jnp.maximum(peak, jnp.max(scores, axis=1, keepdims=True))
        powers = jnp.exp(scores - top)
        fade = jnp.exp(peak - top)
        total = ls[r][:, :1] * fade + jnp.sum(powers, axis=1, keepdims=True)
        mixed = acc[r] * fade + jnp.dot(powers.astype(BF16), nk[1], preferred_element_type=F32)
        result = (mixed / total).astype(BF16)
        for h in range(heads):
            o_pre[pl.ds(pl.multiple_of(r * rows, rows), rows), h * HD:(h + 1) * HD] = (
                result[h * rows:(h + 1) * rows]
            )
        return carry

    lax.fori_loop(0, CHUNKS, finish, 0)

    for send in dec_sends + q_sends + r_sends + key_sends + [cache_send]:
        send.wait_send()
    for r in range(CHUNKS):
        for send in own[r] + onward[r]:
            send.wait_send()


def pool_kernel(pool, fresh, lengths, out, buffer, in_sem, out_sem):
    parts = 4
    size = pool.shape[1] // parts
    pieces = [(c, pl.ds(i * size, size)) for c in range(2) for i in range(parts)]
    reads = [
        pltpu.make_async_copy(pool.at[c, p], buffer.at[c, p], in_sem.at[i])
        for i, (c, p) in enumerate(pieces)
    ]
    writes = [
        pltpu.make_async_copy(buffer.at[c, p], out.at[c, p], out_sem.at[i])
        for i, (c, p) in enumerate(pieces)
    ]
    for copy in reads:
        copy.start()
    for copy in reads:
        copy.wait()
    line = lax.broadcasted_iota(jnp.int32, (16, HD), 0)
    end = jnp.int32(0)
    for s in range(fresh.shape[1]):
        end = end + lengths[s]
        base = pl.multiple_of(lax.div(end, 16) * 16, 16)
        for c in range(2):
            new_row = fresh[c, s:s + 1, :].astype(F32)
            held = buffer[c, pl.ds(base, 16), :].astype(F32)
            buffer[c, pl.ds(base, 16), :] = jnp.where(
                line == end - base, new_row, held
            ).astype(BF16)
        end = end + 1
    for copy in writes:
        copy.start()
    for copy in writes:
        copy.wait()


def body(
    n_tok, dec_tokens, pre_tokens, w_query, w_keyval, b_query, b_keyval,
    dec_pool, owner_slots, dec_lengths, pre_cache, pre_offsets,
):
    dec_rows, width = dec_tokens.shape
    pre_rows = pre_tokens.shape[0]
    q_width = w_query.shape[1]
    heads = q_width // HD
    depth = w_query.shape[0]
    out_width = q_width + 2 * HD
    rows = pre_rows // CHUNKS
    shard = pre_cache.shape[1]
    spread = np.arange(HD // 2, dtype=np.float32) * np.float32(2.0 / HD)
    rates = np.power(np.float32(THETA), -spread).astype(np.float32)
    rates = jnp.asarray(np.concatenate([rates, rates])[None, :])
    hbm = pl.BlockSpec(memory_space=pl.ANY)
    vmem = pl.BlockSpec(memory_space=pltpu.VMEM)
    smem = pl.BlockSpec(memory_space=pltpu.SMEM)
    dma = pltpu.SemaphoreType.DMA
    dec_attn, pre_attn, appended, fresh = pl.pallas_call(
        functools.partial(step_kernel, n_tok),
        name="attention_step",
        out_shape=(
            jax.ShapeDtypeStruct((dec_rows, q_width), BF16),
            jax.ShapeDtypeStruct((pre_rows, q_width), BF16),
            jax.ShapeDtypeStruct((2, pre_rows, HD), BF16),
            jax.ShapeDtypeStruct((2, dec_rows, HD), BF16),
        ),
        in_specs=[hbm, hbm, hbm, hbm, vmem, vmem, hbm, smem, smem, hbm, smem, vmem],
        out_specs=(vmem, vmem, vmem, vmem),
        scratch_shapes=[
            pltpu.VMEM((4, dec_rows, width), BF16),
            pltpu.VMEM((4, pre_rows, width), BF16),
            pltpu.VMEM((depth, out_width), BF16),
            pltpu.VMEM((2 * depth, HD), BF16),
            pltpu.VMEM(dec_pool.shape, BF16),
            pltpu.VMEM((2, 2 * shard, HD), BF16),
            pltpu.VMEM((2, 2 * pre_rows, HD), BF16),
            pltpu.VMEM((CHUNKS, heads * rows, HD), BF16),
            pltpu.VMEM((CHUNKS, heads * rows, HD), F32),
            pltpu.VMEM((CHUNKS, heads * rows, HD), F32),
            pltpu.VMEM((CHUNKS, heads * rows, HD), F32),
            pltpu.VMEM((dec_rows, out_width), BF16),
            pltpu.VMEM((n_tok, dec_rows, out_width), BF16),
            pltpu.VMEM((n_tok, dec_rows, q_width), BF16),
            pltpu.VMEM((n_tok, dec_rows, q_width), BF16),
            dma((6,)),
            dma((3,)), dma((3,)),
            dma((CHUNKS, 4)), dma((CHUNKS, 4)),
            dma((n_tok - 1,)), dma((n_tok - 1,)),
            dma((n_tok - 1,)), dma((n_tok - 1,)),
            dma, dma,
            dma((CHUNKS,)), dma((CHUNKS,)),
        ],
        compiler_params=pltpu.CompilerParams(
            collective_id=0, has_side_effects=True, vmem_limit_bytes=52 * 1024 * 1024
        ),
    )(
        dec_tokens, pre_tokens, w_query, w_keyval.reshape(2 * depth, HD),
        b_query.reshape(1, q_width), b_keyval, dec_pool, owner_slots, dec_lengths,
        pre_cache, pre_offsets, rates,
    )
    new_pool = pl.pallas_call(
        pool_kernel,
        name="append_rows",
        out_shape=jax.ShapeDtypeStruct(dec_pool.shape, BF16),
        in_specs=[hbm, vmem, smem],
        out_specs=hbm,
        scratch_shapes=[pltpu.VMEM(dec_pool.shape, BF16), dma((8,)), dma((8,))],
        compiler_params=pltpu.CompilerParams(vmem_limit_bytes=24 * 1024 * 1024),
    )(dec_pool, fresh, dec_lengths)
    return (dec_attn, pre_attn, new_pool, appended)


def solution(mesh):
    in_specs = (
        P("tok", "kv"),
        P("tok", "kv"),
        P(None, "kv"),
        P(None, None, "kv"),
        P("kv"),
        P(None, "kv"),
        P(None, "tok", "kv"),
        P("tok"),
        P("tok"),
        P(None, "tok", "kv"),
        P(),
    )
    out_specs = (P("tok", "kv"), P("tok", "kv"), P(None, "tok", "kv"), P(None, "tok", "kv"))
    return jax.shard_map(
        functools.partial(body, mesh.shape["tok"]),
        mesh=mesh, in_specs=in_specs, out_specs=out_specs, check_vma=False,
    )
```

time: 156 us -> 60.6 us (0.39)
  blocking collectives: 52.5 us -> 0 us
  Pallas kernels: 0 us -> 50.7 us
  matrix products: 27.4 us -> 0 us
  waiting for transfers between devices: 23.7 us -> 0 us
  other arithmetic: 19.5 us -> 0 us
  between operations: 15.8 us -> 0.66 us
  local copies, waits for them, and re-layouts: 16.2 us -> 8.88 us
    pallas_call x0 -> x2, Pallas kernels: none -> 50.7 us  [the longest x1 46.8 us: body(): pl.pallas_call(functools.partial(step_kernel, n_tok), name='attention_ste...]
    all_gather x3 -> x0, blocking collectives: 42.3 us -> none  [the longest x1 14.2 us: body(): lax.all_gather(dec_query, 'tok', axis=0, tiled=True)]
    dot_general x6 -> x0, matrix products: 27.4 us -> none  [the longest x2 10 us: head_scores(): jnp.einsum('ngd,md->ngm', shaped, key_rows, preferred_element_type=jnp.fl...]
    all_gather x1 -> x0, waiting for transfers between devices: 23.7 us -> none  [body(): columns = lax.all_gather(stacked, 'kv', axis=1, tiled=True)]
    unnamed x1 -> x0, blocking collectives: 10.2 us -> none
    reduce_sum x2 -> x0, other arithmetic: 9.2 us -> none  [head_mix(): totals = jnp.sum(powers, axis=-1)]
    select_n x9 -> x0, other arithmetic: 3.8 us -> none  [the longest x1 1.25 us: body(): jnp.where(is_lower, jnp.concatenate([pre_cache, other_cache], axis=1), jn...]
    scatter x2 -> x0, local copies, waits for them, and re-layouts: 3.3 us -> none  [the longest x1 2.33 us: serve_owner(): cache_pool = cache_pool.at[:, starts + lengths].set(appended)]
  transfers between devices with their start and end apart: 3 -> 0, of which waited for: 1 -> 0; matrix products, arithmetic and copies ran while one was open for 13% -> 0% of each run, Pallas kernels for 0% -> 0%
where the time goes in v1:
time: 60.6 us; the launch traced here: 60.3 us
  Pallas kernels  50.7 us (84%)
  local copies, waits for them, and re-layouts  8.88 us (15%)
  between operations  0.66 us (1%)
    pallas_call x1, Pallas kernels, body(): pl.pallas_call(functools.partial(step_kernel, n_tok), name='attention_ste...  46.8 us
    unnamed x21, local copies, waits for them, and re-layouts  8.19 us
    pallas_call x1, Pallas kernels, body(): pl.pallas_call(pool_kernel, name='append_rows', out_shape=jax.ShapeDtypeS...  3.89 us

profile of v1, /device:TPU:0, one launch (start us, length us, event | category | flops | bytes accessed | tf_op | source)
XLA Modules:
  0.0 60.3 jit_solution(14870682261890611121)
XLA Ops:
  0.6 0.7 %reshape.15.b_q = f32[1,640]{1,0:T(1,128)S(1)} reshape(f32[640]{0:T(1024)} %param.16) | data formatting | bytes 5120 | tf_op jit(solution)/shard_map/reshape | solution.py:418
  1.3 0.0 copy-start.1
  1.3 1.1 %copy-done.1 = bf16[256,1280]{1,0:T(8,128)(2,1)S(1)} copy-done((bf16[256,1280]{1,0:T(8,128)(2,1)S(1)}, bf16[256,1280]{1,0:T(8,128)(2,1)}, u32[]{:S(2)}) %copy-start.1) | copy-done | bytes 655384
  2.4 0.0 copy-start.2
  2.4 1.0 %copy-done.2 = bf16[2,1024,128]{2,1,0:T(8,128)(2,1)S(1)} copy-done((bf16[2,1024,128]{2,1,0:T(8,128)(2,1)S(1)}, bf16[2,1024,128]{2,1,0:T(8,128)(2,1)}, u32[]{:S(2)}) %copy-start.2) | copy-done | bytes 524312
  3.5 0.0 copy-start.3
  3.5 0.8 %copy-done.3 = bf16[16,1280]{1,0:T(8,128)(2,1)S(1)} copy-done((bf16[16,1280]{1,0:T(8,128)(2,1)S(1)}, bf16[16,1280]{1,0:T(8,128)(2,1)}, u32[]{:S(2)}) %copy-start.3) | copy-done | bytes 40984
  4.2 0.0 copy-start.4
  4.2 0.7 %copy-done.4 = s32[16]{0:T(128)S(1)} copy-done((s32[16]{0:T(128)S(1)}, s32[16]{0:T(128)}, u32[]{:S(2)}) %copy-start.4) | copy-done | bytes 88
  4.9 0.0 copy-start.5
  4.9 0.7 %copy-done.5 = f32[2,128]{1,0:T(2,128)S(1)} copy-done((f32[2,128]{1,0:T(2,128)S(1)}, f32[2,128]{1,0:T(2,128)}, u32[]{:S(2)}) %copy-start.5) | copy-done | bytes 1048
  5.6 0.0 copy-start.6
  5.6 0.7 %copy-done.6 = s32[16]{0:T(128)S(1)} copy-done((s32[16]{0:T(128)S(1)}, s32[16]{0:T(128)}, u32[]{:S(2)}) %copy-start.6) | copy-done | bytes 88
  6.2 0.0 copy-start.7
  6.2 0.7 %copy-done.7 = s32[4]{0:T(128)S(1)} copy-done((s32[4]{0:T(128)S(1)}, s32[4]{0:T(128)}, u32[]{:S(2)}) %copy-start.7) | copy-done | bytes 40
  6.9 0.0 copy-start.8
  6.9 0.7 %copy-done.8 = f32[1,128]{1,0:T(1,128)S(1)} copy-done((f32[1,128]{1,0:T(1,128)S(1)}, f32[1,128]{1,0:T(1,128)}, u32[]{:S(2)}) %copy-start.8) | copy-done | bytes 536
  7.5 0.0 copy-start
  7.5 46.8 %attention_step.1 = (bf16[16,640]{1,0:T(8,128)(2,1)S(1)}, bf16[256,640]{1,0:T(8,128)(2,1)S(1)}, bf16[2,256,128]{2,1,0:T(8,128)(2,1)S(1)}, bf16[2,16,128]{2,1,0:T(8,128)(2,1)S(1)}) custom-call(bf16[16,1280]{1,0:T(8,128)(2,1)S(1)} %copy-done.3, bf16[256,1280]{1,0:T(8,128)(2,1)S(1)} %copy-done.1, bf16[5120,640]{1,0:T(8,128)(2,1)} %w_q.1, ...), custom_call_target="tpu_custom_call" | custom-call | tf_op jit(solution)/shard_map/attention_step/pallas_call | solution.py:378
  54.4 0.0 copy-done
  54.4 3.9 %append_rows.1 = bf16[2,12288,128]{2,1,0:T(8,128)(2,1)} custom-call(bf16[2,12288,128]{2,1,0:T(8,128)(2,1)S(1)} %copy-done, bf16[2,16,128]{2,1,0:T(8,128)(2,1)S(1)} %get-tuple-element.10.fresh, s32[16]{0:T(128)S(1)} %copy-done.4), custom_call_target="tpu_custom_call" | custom-call | tf_op jit(solution)/shard_map/append_rows/pallas_call | solution.py:421
  58.3 0.6 %copy.19 = bf16[16,640]{1,0:T(8,128)(2,1)} copy(bf16[16,640]{1,0:T(8,128)(2,1)S(1)} %get-tuple-element.16) | data formatting | bytes 40960
  58.9 0.7 %copy.20 = bf16[256,640]{1,0:T(8,128)(2,1)} copy(bf16[256,640]{1,0:T(8,128)(2,1)S(1)} %get-tuple-element.17) | data formatting | bytes 655360
  59.6 0.7 %copy.21 = bf16[2,256,128]{2,1,0:T(8,128)(2,1)} copy(bf16[2,256,128]{2,1,0:T(8,128)(2,1)S(1)} %get-tuple-element.19) | data formatting | bytes 262144
Async XLA Ops:
  1.3 1.1 %copy-start.1 = (bf16[256,1280]{1,0:T(8,128)(2,1)S(1)}, bf16[256,1280]{1,0:T(8,128)(2,1)}, u32[]{:S(2)}) copy-start(bf16[256,1280]{1,0:T(8,128)(2,1)} %pre_x.1) | copy-start | bytes 1966084
  2.4 1.0 %copy-start.2 = (bf16[2,1024,128]{2,1,0:T(8,128)(2,1)S(1)}, bf16[2,1024,128]{2,1,0:T(8,128)(2,1)}, u32[]{:S(2)}) copy-start(bf16[2,1024,128]{2,1,0:T(8,128)(2,1)} %cache.1) | copy-start | bytes 1572868
  3.5 0.8 %copy-start.3 = (bf16[16,1280]{1,0:T(8,128)(2,1)S(1)}, bf16[16,1280]{1,0:T(8,128)(2,1)}, u32[]{:S(2)}) copy-start(bf16[16,1280]{1,0:T(8,128)(2,1)} %dec_x.1) | copy-start | bytes 122884
  4.2 0.7 %copy-start.4 = (s32[16]{0:T(128)S(1)}, s32[16]{0:T(128)}, u32[]{:S(2)}) copy-start(s32[16]{0:T(128)} %lengths.3) | copy-start | bytes 196
  4.9 0.7 %copy-start.5 = (f32[2,128]{1,0:T(2,128)S(1)}, f32[2,128]{1,0:T(2,128)}, u32[]{:S(2)}) copy-start(f32[2,128]{1,0:T(2,128)} %b_kv.1) | copy-start | bytes 3076
  5.6 0.7 %copy-start.6 = (s32[16]{0:T(128)S(1)}, s32[16]{0:T(128)}, u32[]{:S(2)}) copy-start(s32[16]{0:T(128)} %slots.1) | copy-start | bytes 196
  6.2 0.7 %copy-start.7 = (s32[4]{0:T(128)S(1)}, s32[4]{0:T(128)}, u32[]{:S(2)}) copy-start(s32[4]{0:T(128)} %offsets.1) | copy-start | bytes 52
  6.9 0.7 %copy-start.8 = (f32[1,128]{1,0:T(1,128)S(1)}, f32[1,128]{1,0:T(1,128)}, u32[]{:S(2)}) copy-start(f32[1,128]{1,0:T(1,128)} %constant.2.clone.rates) | copy-start | bytes 1540
  7.5 46.8 %copy-start = (bf16[2,12288,128]{2,1,0:T(8,128)(2,1)S(1)}, bf16[2,12288,128]{2,1,0:T(8,128)(2,1)}, u32[]{:S(2)}) copy-start(bf16[2,12288,128]{2,1,0:T(8,128)(2,1)} %pool.3) | copy-start | bytes 18874372

commit v2 on v1

--- a/solution.py
+++ b/solution.py
@@ -12,6 +12,8 @@
 THETA = 1000000.0
 MESH = pl.DeviceIdType.MESH
 CHUNKS = 4
+GROUPS = 2
+LOG2E = 1.4426950408889634
 F32 = jnp.float32
 BF16 = jnp.bfloat16
 
@@ -26,9 +28,11 @@
 
 def step_kernel(
     n_tok,
-    dec_x, pre_x, w_q, w_kv, b_q, b_kv, pool, slots, lengths, cache, offsets, rates,
+    dec_x, pre_x, w_q, w_kv, b_q_in, b_kv_in, pool, slots_in, lengths_in, cache, offsets_in,
+    rates_in,
     o_dec, o_pre, o_kv, o_new,
     xd, xp, w, raw, kvpool, hist, nk, qs, ms, ls, acc, dq_own, dq_all, dr_send, dr_recv,
+    b_q, b_kv, slots, lengths, offsets, rates,
     l_sem, ds_sem, dr_sem, ps_sem, pr_sem, qs_sem, qr_sem, rs_sem, rr_sem,
     cs_sem, cr_sem, ks_sem, kr_sem,
 ):
@@ -46,7 +50,7 @@
     rows = pre_rows // CHUNKS
     mid = rows // 2
     shard = cache.shape[1]
-    scale = HD ** -0.5
+    scale = HD ** -0.5 * LOG2E
 
     loads = [
         pltpu.make_async_copy(w_kv, raw, l_sem.at[0]),
@@ -57,9 +61,16 @@
             cache, hist.at[:, pl.ds(pl.multiple_of(half * shard, shard), shard)], l_sem.at[4]
         ),
         pltpu.make_async_copy(pool, kvpool, l_sem.at[5]),
+        pltpu.make_async_copy(b_q_in, b_q, l_sem.at[6]),
+        pltpu.make_async_copy(b_kv_in, b_kv, l_sem.at[7]),
+        pltpu.make_async_copy(slots_in, slots, l_sem.at[8]),
+        pltpu.make_async_copy(lengths_in, lengths, l_sem.at[9]),
+        pltpu.make_async_copy(offsets_in, offsets, l_sem.at[10]),
+        pltpu.make_async_copy(rates_in, rates, l_sem.at[11]),
     ]
-    for load in loads:
-        load.start()
+    for i, load in enumerate(loads):
+        if i != 5:
+            load.start()
 
     barrier = pltpu.get_barrier_semaphore()
     for peer in (px, py, pd):
@@ -116,21 +127,30 @@
                 send.start()
 
     loads[0].wait()
-    block = 512
+    block, beside = 256, 8
     row = lax.broadcasted_iota(jnp.int32, (block, block), 0)
     col = lax.broadcasted_iota(jnp.int32, (block, block), 1)
     wanted = jnp.where(row < block // 2, 2 * row, 2 * row - block + 1)
     permute = jnp.where(col == wanted, 1.0, 0.0).astype(BF16)
 
     def part_weights(i, carry):
-        tile = raw[pl.ds(pl.multiple_of(i * block, block), block), :]
-        parted = jnp.dot(permute, tile, preferred_element_type=F32).astype(BF16)
-        where = pl.ds(pl.multiple_of(i * (block // 2), block // 2), block // 2)
-        w[where, pl.ds(q_width, HD)] = parted[: block // 2]
-        w[where, pl.ds(q_width + HD, HD)] = parted[block // 2:]
+        tiles = jnp.concatenate(
+            [raw[pl.ds(pl.multiple_of((i * beside + j) * block, block), block), :]
+             for j in range(beside)],
+            axis=1,
+        )
+        parted = jnp.dot(permute, tiles, preferred_element_type=F32).astype(BF16)
+        for j in range(beside):
+            half_block = block // 2
+            where = pl.ds(pl.multiple_of((i * beside + j) * half_block, half_block), half_block)
+            w[where, pl.ds(q_width, HD)] = parted[:half_block, j * HD:(j + 1) * HD]
+            w[where, pl.ds(q_width + HD, HD)] = parted[half_block:, j * HD:(j + 1) * HD]
         return carry
 
-    lax.fori_loop(0, raw.shape[0] // block, part_weights, 0)
+    lax.fori_loop(0, raw.shape[0] // (block * beside), part_weights, 0)
+    pump(0)
+    for load in loads[6:]:
+        load.wait()
 
     def project(x_ref, start, amount):
         def add(s, total):
@@ -141,10 +161,11 @@
             )
 
         total = lax.fori_loop(0, 4, add, jnp.zeros((amount, q_width + 2 * HD), F32))
-        bias = jnp.concatenate([b_q[...], b_kv[0:1, :], b_kv[1:2, :]], axis=1)
+        bias = jnp.concatenate([b_q[...].reshape(1, q_width), b_kv[0:1, :], b_kv[1:2, :]], axis=1)
         return total + bias
 
     loads[1].wait()
+    loads[5].start()
     loads[2].wait()
     for send in dec_sends:
         send.wait_recv()
@@ -158,8 +179,8 @@
         send.start()
     dq_all[tok] = dq_own[...]
 
-    pump(0)
     pump(1)
+    pump(2)
 
     for send in q_sends:
         send.wait_recv()
@@ -205,7 +226,7 @@
     same = slot_of == lax.broadcasted_iota(jnp.int32, (stacked, dec_rows), 1)
     scores = jnp.where(same, dot_nt(turned, fresh_k) * scale, -jnp.inf)
     peak = jnp.max(scores, axis=1, keepdims=True)
-    powers = jnp.exp(scores - peak)
+    powers = jnp.exp2(scores - peak)
     total = jnp.sum(powers, axis=1, keepdims=True)
     mixed = jnp.dot(powers.astype(BF16), fresh_v, preferred_element_type=F32)
     loads[5].wait()
@@ -218,8 +239,8 @@
         scores = dot_nt(turned, kvpool[0, where, :]) * scale
         scores = jnp.where((spots >= first) & (spots < last), scores, -jnp.inf)
         top = jnp.maximum(peak, jnp.max(scores, axis=1, keepdims=True))
-        powers = jnp.exp(scores - top)
-        fade = jnp.exp(peak - top)
+        powers = jnp.exp2(scores - top)
+        fade = jnp.exp2(peak - top)
         total = total * fade + jnp.sum(powers, axis=1, keepdims=True)
         mixed = mixed * fade + jnp.dot(
             powers.astype(BF16), kvpool[1, where, :], preferred_element_type=F32
@@ -243,16 +264,18 @@
     for send in r_sends:
         send.start()
     dr_recv[tok] = dr_send[tok]
-    pump(2)
+    pump(3)
 
     offset = offsets[lax.div(tok, 2)]
     loads[3].wait()
     loads[4].wait()
     cache_send.wait_recv()
     key_sends = []
-    for r in range(CHUNKS):
-        for send in onward[r]:
-            send.wait_recv()
+    rows = pre_rows // GROUPS
+    for r in range(GROUPS):
+        for piece in range(r * CHUNKS // GROUPS, (r + 1) * CHUNKS // GROUPS):
+            for send in onward[piece]:
+                send.wait_recv()
         value = project(xp, r * rows, rows)
         place = pl.multiple_of(half * pre_rows + r * rows, rows)
         positions = offset + place + lax.broadcasted_iota(jnp.int32, (rows, HD), 0)
@@ -273,13 +296,11 @@
         send = remote(part, part, ks_sem.at[r], kr_sem.at[r], (kv, mate))
         send.start()
         key_sends.append(send)
-        if r == 0:
-            pump(3)
         scores = dot_nt(queries, hist[0]) * scale
         cached = lax.broadcasted_iota(jnp.int32, (1, 2 * shard), 1) < offset
         scores = jnp.where(cached, scores, -jnp.inf)
         peak = jnp.max(scores, axis=1, keepdims=True)
-        powers = jnp.exp(scores - peak)
+        powers = jnp.exp2(scores - peak)
         total = jnp.sum(powers, axis=1, keepdims=True)
         acc[r] = jnp.dot(powers.astype(BF16), hist[1], preferred_element_type=F32)
         ms[r] = jnp.broadcast_to(peak, (heads * rows, HD))
@@ -302,8 +323,8 @@
         scores = jnp.where(later <= inner + (half * pre_rows + r * rows), scores, -jnp.inf)
         peak = ms[r][:, :1]
         top = jnp.maximum(peak, jnp.max(scores, axis=1, keepdims=True))
-        powers = jnp.exp(scores - top)
-        fade = jnp.exp(peak - top)
+        powers = jnp.exp2(scores - top)
+        fade = jnp.exp2(peak - top)
         total = ls[r][:, :1] * fade + jnp.sum(powers, axis=1, keepdims=True)
         mixed = acc[r] * fade + jnp.dot(powers.astype(BF16), nk[1], preferred_element_type=F32)
         result = (mixed / total).astype(BF16)
@@ -313,7 +334,7 @@
             )
         return carry
 
-    lax.fori_loop(0, CHUNKS, finish, 0)
+    lax.fori_loop(0, GROUPS, finish, 0)
 
     for send in dec_sends + q_sends + r_sends + key_sends + [cache_send]:
         send.wait_send()
@@ -322,7 +343,10 @@
             send.wait_send()
 
 
-def pool_kernel(pool, fresh, lengths, out, buffer, in_sem, out_sem):
+def pool_kernel(
+    pool, fresh_in, lengths_in, dec_in, pre_in, kv_in, out, dec_out, pre_out, kv_out,
+    buffer, fresh, lengths, dec_b, pre_b, kv_b, in_sem, out_sem,
+):
     parts = 4
     size = pool.shape[1] // parts
     pieces = [(c, pl.ds(i * size, size)) for c in range(2) for i in range(parts)]
@@ -334,6 +358,13 @@
         pltpu.make_async_copy(buffer.at[c, p], out.at[c, p], out_sem.at[i])
         for i, (c, p) in enumerate(pieces)
     ]
+    count = len(pieces)
+    rest = ((dec_in, dec_b, dec_out), (pre_in, pre_b, pre_out), (kv_in, kv_b, kv_out))
+    for i, (source, held, target) in enumerate(rest):
+        reads.append(pltpu.make_async_copy(source, held, in_sem.at[count + i]))
+        writes.append(pltpu.make_async_copy(held, target, out_sem.at[count + i]))
+    reads.append(pltpu.make_async_copy(fresh_in, fresh, in_sem.at[count + 3]))
+    reads.append(pltpu.make_async_copy(lengths_in, lengths, in_sem.at[count + 4]))
     for copy in reads:
         copy.start()
     for copy in reads:
@@ -366,14 +397,13 @@
     heads = q_width // HD
     depth = w_query.shape[0]
     out_width = q_width + 2 * HD
-    rows = pre_rows // CHUNKS
+    rows = pre_rows // GROUPS
     shard = pre_cache.shape[1]
     spread = np.arange(HD // 2, dtype=np.float32) * np.float32(2.0 / HD)
     rates = np.power(np.float32(THETA), -spread).astype(np.float32)
     rates = jnp.asarray(np.concatenate([rates, rates])[None, :])
     hbm = pl.BlockSpec(memory_space=pl.ANY)
     vmem = pl.BlockSpec(memory_space=pltpu.VMEM)
-    smem = pl.BlockSpec(memory_space=pltpu.SMEM)
     dma = pltpu.SemaphoreType.DMA
     dec_attn, pre_attn, appended, fresh = pl.pallas_call(
         functools.partial(step_kernel, n_tok),
@@ -384,7 +414,7 @@
             jax.ShapeDtypeStruct((2, pre_rows, HD), BF16),
             jax.ShapeDtypeStruct((2, dec_rows, HD), BF16),
         ),
-        in_specs=[hbm, hbm, hbm, hbm, vmem, vmem, hbm, smem, smem, hbm, smem, vmem],
+        in_specs=[hbm] * 12,
         out_specs=(vmem, vmem, vmem, vmem),
         scratch_shapes=[
             pltpu.VMEM((4, dec_rows, width), BF16),
@@ -394,39 +424,55 @@
             pltpu.VMEM(dec_pool.shape, BF16),
             pltpu.VMEM((2, 2 * shard, HD), BF16),
             pltpu.VMEM((2, 2 * pre_rows, HD), BF16),
-            pltpu.VMEM((CHUNKS, heads * rows, HD), BF16),
-            pltpu.VMEM((CHUNKS, heads * rows, HD), F32),
-            pltpu.VMEM((CHUNKS, heads * rows, HD), F32),
-            pltpu.VMEM((CHUNKS, heads * rows, HD), F32),
+            pltpu.VMEM((GROUPS, heads * rows, HD), BF16),
+            pltpu.VMEM((GROUPS, heads * rows, HD), F32),
+            pltpu.VMEM((GROUPS, heads * rows, HD), F32),
+            pltpu.VMEM((GROUPS, heads * rows, HD), F32),
             pltpu.VMEM((dec_rows, out_width), BF16),
             pltpu.VMEM((n_tok, dec_rows, out_width), BF16),
             pltpu.VMEM((n_tok, dec_rows, q_width), BF16),
             pltpu.VMEM((n_tok, dec_rows, q_width), BF16),
-            dma((6,)),
+            pltpu.VMEM((q_width,), F32),
+            pltpu.VMEM((2, HD), F32),
+            pltpu.SMEM(owner_slots.shape, jnp.int32),
+            pltpu.SMEM(dec_lengths.shape, jnp.int32),
+            pltpu.SMEM(pre_offsets.shape, jnp.int32),
+            pltpu.VMEM((1, HD), F32),
+            dma((12,)),
             dma((3,)), dma((3,)),
             dma((CHUNKS, 4)), dma((CHUNKS, 4)),
             dma((n_tok - 1,)), dma((n_tok - 1,)),
             dma((n_tok - 1,)), dma((n_tok - 1,)),
             dma, dma,
-            dma((CHUNKS,)), dma((CHUNKS,)),
+            dma((GROUPS,)), dma((GROUPS,)),
         ],
         compiler_params=pltpu.CompilerParams(
-            collective_id=0, has_side_effects=True, vmem_limit_bytes=52 * 1024 * 1024
+            collective_id=0, has_side_effects=True, vmem_limit_bytes=64 * 1024 * 1024
         ),
     )(
         dec_tokens, pre_tokens, w_query, w_keyval.reshape(2 * depth, HD),
-        b_query.reshape(1, q_width), b_keyval, dec_pool, owner_slots, dec_lengths,
+        b_query, b_keyval, dec_pool, owner_slots, dec_lengths,
         pre_cache, pre_offsets, rates,
     )
-    new_pool = pl.pallas_call(
+    rest = (dec_attn, pre_attn, appended)
+    new_pool, dec_attn, pre_attn, appended = pl.pallas_call(
         pool_kernel,
         name="append_rows",
-        out_shape=jax.ShapeDtypeStruct(dec_pool.shape, BF16),
-        in_specs=[hbm, vmem, smem],
-        out_specs=hbm,
-        scratch_shapes=[pltpu.VMEM(dec_pool.shape, BF16), dma((8,)), dma((8,))],
-        compiler_params=pltpu.CompilerParams(vmem_limit_bytes=24 * 1024 * 1024),
-    )(dec_pool, fresh, dec_lengths)
+        out_shape=(
+            jax.ShapeDtypeStruct(dec_pool.shape, BF16),
+            *(jax.ShapeDtypeStruct(value.shape, BF16) for value in rest),
+        ),
+        in_specs=[hbm] * 6,
+        out_specs=[hbm] * 4,
+        scratch_shapes=[
+            pltpu.VMEM(dec_pool.shape, BF16),
+            pltpu.VMEM(fresh.shape, BF16),
+            pltpu.SMEM(dec_lengths.shape, jnp.int32),
+            *(pltpu.VMEM(value.shape, BF16) for value in rest),
+            dma((13,)), dma((11,)),
+        ],
+        compiler_params=pltpu.CompilerParams(vmem_limit_bytes=64 * 1024 * 1024),
+    )(dec_pool, fresh, dec_lengths, *rest)
     return (dec_attn, pre_attn, new_pool, appended)
 
 

time: 60.6 us -> 53.1 us (0.88)
  local copies, waits for them, and re-layouts: 8.88 us -> 0 us
  Pallas kernels: 50.7 us -> 52.4 us
    unnamed x21 -> x0, local copies, waits for them, and re-layouts: 8.19 us -> none
    pallas_call x1, Pallas kernels: 3.89 us -> 6 us  [body(): pl.pallas_call(pool_kernel, name='append_rows', out_shape=(jax.ShapeDtype...]
    reshape x1 -> x0, local copies, waits for them, and re-layouts: 0.69 us -> none  [body(): b_query.reshape(1, q_width)]
where the time goes in v2:
time: 53.1 us; the launch traced here: 53 us
  Pallas kernels  52.4 us (99%)
  between operations  0.64 us (1%)
    pallas_call x1, Pallas kernels, body(): pl.pallas_call(functools.partial(step_kernel, n_tok), name='attention_ste...  46.4 us
    pallas_call x1, Pallas kernels, body(): pl.pallas_call(pool_kernel, name='append_rows', out_shape=(jax.ShapeDtype...  6 us

profile of v2, /device:TPU:0, one launch (start us, length us, event | category | flops | bytes accessed | tf_op | source)
XLA Modules:
  0.0 53.0 jit_solution(13675327226195576479)
XLA Ops:
  0.6 46.4 %attention_step.1 = (bf16[16,640]{1,0:T(8,128)(2,1)}, bf16[256,640]{1,0:T(8,128)(2,1)}, bf16[2,256,128]{2,1,0:T(8,128)(2,1)}, bf16[2,16,128]{2,1,0:T(8,128)(2,1)}) custom-call(bf16[16,1280]{1,0:T(8,128)(2,1)} %dec_x.1, bf16[256,1280]{1,0:T(8,128)(2,1)} %pre_x.1, bf16[5120,640]{1,0:T(8,128)(2,1)} %w_q.1, bf16[10240,128]{1,0:T(8,128)(2,1)} %bitcast.1, ...), custom_call_target="tpu_custom_call" | custom-call | tf_op jit(solution)/shard_map/attention_step/pallas_call | solution.py:408
  47.0 6.0 %append_rows.1 = (bf16[2,12288,128]{2,1,0:T(8,128)(2,1)}, bf16[16,640]{1,0:T(8,128)(2,1)}, bf16[256,640]{1,0:T(8,128)(2,1)}, bf16[2,256,128]{2,1,0:T(8,128)(2,1)}) custom-call(bf16[2,12288,128]{2,1,0:T(8,128)(2,1)} %pool.3, bf16[2,16,128]{2,1,0:T(8,128)(2,1)} %get-tuple-element.12.fresh_in, s32[16]{0:T(128)} %lengths_in.3, ...), custom_call_target="tpu_custom_call" | custom-call | tf_op jit(solution)/shard_map/append_rows/pallas_call | solution.py:458

commit v3 on v2

--- a/solution.py
+++ b/solution.py
@@ -26,13 +26,25 @@
     return lax.dot_general(a, b, (((1,), (1,)), ((), ())), preferred_element_type=F32)
 
 
+def lane_max(run, value):
+    for j in range(value.shape[1] // HD):
+        run = jnp.maximum(run, value[:, j * HD:(j + 1) * HD])
+    return run
+
+
+def lane_sum(run, value):
+    for j in range(value.shape[1] // HD):
+        run = run + value[:, j * HD:(j + 1) * HD]
+    return run
+
+
 def step_kernel(
     n_tok,
     dec_x, pre_x, w_q, w_kv, b_q_in, b_kv_in, pool, slots_in, lengths_in, cache, offsets_in,
     rates_in,
     o_dec, o_pre, o_kv, o_new,
     xd, xp, w, raw, kvpool, hist, nk, qs, ms, ls, acc, dq_own, dq_all, dr_send, dr_recv,
-    b_q, b_kv, slots, lengths, offsets, rates,
+    b_q, b_kv, slots, lengths, offsets, rates, marks, long_marks,
     l_sem, ds_sem, dr_sem, ps_sem, pr_sem, qs_sem, qr_sem, rs_sem, rr_sem,
     cs_sem, cr_sem, ks_sem, kr_sem,
 ):
@@ -152,24 +164,24 @@
     for load in loads[6:]:
         load.wait()
 
-    def project(x_ref, start, amount):
-        def add(s, total):
-            return total + jnp.dot(
-                x_ref[s, pl.ds(start, amount), :],
-                w[pl.ds(pl.multiple_of(s * width, width), width), :],
+    def project(x_ref, start, amount, arrive):
+        total = jnp.concatenate([b_q[...].reshape(1, q_width), b_kv[0:1, :], b_kv[1:2, :]], axis=1)
+        for source in (kv, px, py, pd):
+            if source is pd:
+                arrive()
+            total = total + jnp.dot(
+                x_ref[source, pl.ds(start, amount), :],
+                w[pl.ds(pl.multiple_of(source * width, width), width), :],
                 preferred_element_type=F32,
             )
-
-        total = lax.fori_loop(0, 4, add, jnp.zeros((amount, q_width + 2 * HD), F32))
-        bias = jnp.concatenate([b_q[...].reshape(1, q_width), b_kv[0:1, :], b_kv[1:2, :]], axis=1)
-        return total + bias
+        return total
 
     loads[1].wait()
     loads[5].start()
     loads[2].wait()
     for send in dec_sends:
         send.wait_recv()
-    dq_own[...] = project(xd, 0, dec_rows).astype(BF16)
+    dq_own[...] = project(xd, 0, dec_rows, lambda: None).astype(BF16)
     q_sends = [
         remote(dq_own, dq_all.at[tok], qs_sem.at[d - 1], qr_sem.at[d - 1],
                (kv, lax.rem(tok + d, n_tok)))
@@ -230,24 +242,38 @@
     total = jnp.sum(powers, axis=1, keepdims=True)
     mixed = jnp.dot(powers.astype(BF16), fresh_v, preferred_element_type=F32)
     loads[5].wait()
-    tile = 2048
-
-    def visit(t, carry):
-        peak, total, mixed = carry
-        where = pl.ds(pl.multiple_of(t * tile, tile), tile)
-        spots = t * tile + lax.broadcasted_iota(jnp.int32, (stacked, tile), 1)
-        scores = dot_nt(turned, kvpool[0, where, :]) * scale
-        scores = jnp.where((spots >= first) & (spots < last), scores, -jnp.inf)
-        top = jnp.maximum(peak, jnp.max(scores, axis=1, keepdims=True))
-        powers = jnp.exp2(scores - top)
-        fade = jnp.exp2(peak - top)
-        total = total * fade + jnp.sum(powers, axis=1, keepdims=True)
-        mixed = mixed * fade + jnp.dot(
-            powers.astype(BF16), kvpool[1, where, :], preferred_element_type=F32
-        )
-        return top, total, mixed
-
-    peak, total, mixed = lax.fori_loop(0, pool.shape[1] // tile, visit, (peak, total, mixed))
+    wide, tile = 2048, 512
+    strides = pool.shape[1] // wide
+
+    def score(t, run):
+        for j in range(wide // tile):
+            start = pl.multiple_of(t * wide + j * tile, tile)
+            spots = start + lax.broadcasted_iota(jnp.int32, (stacked, tile), 1)
+            value = dot_nt(turned, kvpool[0, pl.ds(start, tile), :]) * scale
+            value = jnp.where((spots >= first) & (spots < last), value, -jnp.inf)
+            long_marks[:, pl.ds(start, tile)] = value
+            run = lane_max(run, value)
+        return run
+
+    run = lax.fori_loop(0, strides, score, jnp.broadcast_to(peak, (stacked, HD)))
+    top = jnp.max(run, axis=1, keepdims=True)
+    fade = jnp.exp2(peak - top)
+
+    def mix(t, carry):
+        sums, mixed = carry
+        for j in range(wide // tile):
+            start = pl.multiple_of(t * wide + j * tile, tile)
+            powers = jnp.exp2(long_marks[:, pl.ds(start, tile)] - top)
+            sums = lane_sum(sums, powers)
+            mixed = mixed + jnp.dot(
+                powers.astype(BF16), kvpool[1, pl.ds(start, tile), :], preferred_element_type=F32
+            )
+        return sums, mixed
+
+    sums, mixed = lax.fori_loop(
+        0, strides, mix, (jnp.zeros((stacked, HD), F32), mixed * fade)
+    )
+    total = total * fade + jnp.sum(sums, axis=1, keepdims=True)
     result = (mixed / total).astype(BF16)
     result = jnp.concatenate(
         [result[h * dec_rows:(h + 1) * dec_rows] for h in range(heads)], axis=1
@@ -272,11 +298,15 @@
     cache_send.wait_recv()
     key_sends = []
     rows = pre_rows // GROUPS
+    span = 256
     for r in range(GROUPS):
-        for piece in range(r * CHUNKS // GROUPS, (r + 1) * CHUNKS // GROUPS):
-            for send in onward[piece]:
-                send.wait_recv()
-        value = project(xp, r * rows, rows)
+
+        def arrive():
+            for piece in range(r * CHUNKS // GROUPS, (r + 1) * CHUNKS // GROUPS):
+                for send in onward[piece]:
+                    send.wait_recv()
+
+        value = project(xp, r * rows, rows, arrive)
         place = pl.multiple_of(half * pre_rows + r * rows, rows)
         positions = offset + place + lax.broadcasted_iota(jnp.int32, (rows, HD), 0)
         angles = positions.astype(F32) * rates[...]
@@ -296,15 +326,33 @@
         send = remote(part, part, ks_sem.at[r], kr_sem.at[r], (kv, mate))
         send.start()
         key_sends.append(send)
-        scores = dot_nt(queries, hist[0]) * scale
-        cached = lax.broadcasted_iota(jnp.int32, (1, 2 * shard), 1) < offset
-        scores = jnp.where(cached, scores, -jnp.inf)
-        peak = jnp.max(scores, axis=1, keepdims=True)
-        powers = jnp.exp2(scores - peak)
-        total = jnp.sum(powers, axis=1, keepdims=True)
-        acc[r] = jnp.dot(powers.astype(BF16), hist[1], preferred_element_type=F32)
-        ms[r] = jnp.broadcast_to(peak, (heads * rows, HD))
-        ls[r] = jnp.broadcast_to(total, (heads * rows, HD))
+
+        def cached_head(h, carry):
+            where = pl.ds(pl.multiple_of(h * rows, rows), rows)
+            query = qs[r, where, :]
+            run = jnp.full((rows, HD), -jnp.inf, F32)
+            for t in range(2 * shard // span):
+                cached = lax.broadcasted_iota(jnp.int32, (1, span), 1) + t * span < offset
+                value = dot_nt(query, hist[0, t * span:(t + 1) * span, :]) * scale
+                value = jnp.where(cached, value, -jnp.inf)
+                marks[:, t * span:(t + 1) * span] = value
+                run = lane_max(run, value)
+            top = jnp.max(run, axis=1, keepdims=True)
+            sums = jnp.zeros((rows, HD), F32)
+            mixed = jnp.zeros((rows, HD), F32)
+            for t in range(2 * shard // span):
+                powers = jnp.exp2(marks[:, t * span:(t + 1) * span] - top)
+                sums = lane_sum(sums, powers)
+                mixed = mixed + jnp.dot(
+                    powers.astype(BF16), hist[1, t * span:(t + 1) * span, :],
+                    preferred_element_type=F32,
+                )
+            acc[r, where, :] = mixed
+            ms[r, where, :] = jnp.broadcast_to(top, (rows, HD))
+            ls[r, where, :] = jnp.broadcast_to(jnp.sum(sums, axis=1, keepdims=True), (rows, HD))
+            return carry
+
+        lax.fori_loop(0, heads, cached_head, 0)
 
     for send in r_sends:
         send.wait_recv()
@@ -315,26 +363,35 @@
 
     for send in key_sends:
         send.wait_recv()
-    inner = lax.rem(lax.broadcasted_iota(jnp.int32, (heads * rows, 1), 0), rows)
-    later = lax.broadcasted_iota(jnp.int32, (heads * rows, 2 * pre_rows), 1)
-
-    def finish(r, carry):
-        scores = dot_nt(qs[r], nk[0]) * scale
-        scores = jnp.where(later <= inner + (half * pre_rows + r * rows), scores, -jnp.inf)
-        peak = ms[r][:, :1]
-        top = jnp.maximum(peak, jnp.max(scores, axis=1, keepdims=True))
-        powers = jnp.exp2(scores - top)
-        fade = jnp.exp2(peak - top)
-        total = ls[r][:, :1] * fade + jnp.sum(powers, axis=1, keepdims=True)
-        mixed = acc[r] * fade + jnp.dot(powers.astype(BF16), nk[1], preferred_element_type=F32)
-        result = (mixed / total).astype(BF16)
+    inner = lax.broadcasted_iota(jnp.int32, (rows, span), 0)
+    later = lax.broadcasted_iota(jnp.int32, (rows, span), 1)
+
+    for r in range(GROUPS):
         for h in range(heads):
-            o_pre[pl.ds(pl.multiple_of(r * rows, rows), rows), h * HD:(h + 1) * HD] = (
-                result[h * rows:(h + 1) * rows]
-            )
-        return carry
-
-    lax.fori_loop(0, GROUPS, finish, 0)
+            part = slice(h * rows, (h + 1) * rows)
+            query = qs[r, part, :]
+            peak = ms[r, part, :]
+            run = peak
+            values = []
+            for t in range(2 * pre_rows // span):
+                value = dot_nt(query, nk[0, t * span:(t + 1) * span, :]) * scale
+                allowed = later + t * span <= inner + (half * pre_rows + r * rows)
+                value = jnp.where(allowed, value, -jnp.inf)
+                values.append(value)
+                run = lane_max(run, value)
+            top = jnp.max(run, axis=1, keepdims=True)
+            fade = jnp.exp2(peak - top)
+            mixed = acc[r, part, :] * fade
+            sums = jnp.zeros((rows, HD), F32)
+            for t, value in enumerate(values):
+                powers = jnp.exp2(value - top)
+                sums = lane_sum(sums, powers)
+                mixed = mixed + jnp.dot(
+                    powers.astype(BF16), nk[1, t * span:(t + 1) * span, :],
+                    preferred_element_type=F32,
+                )
+            total = ls[r, part, :] * fade + jnp.sum(sums, axis=1, keepdims=True)
+            o_pre[r * rows:(r + 1) * rows, h * HD:(h + 1) * HD] = (mixed / total).astype(BF16)
 
     for send in dec_sends + q_sends + r_sends + key_sends + [cache_send]:
         send.wait_send()
@@ -414,7 +471,7 @@
             jax.ShapeDtypeStruct((2, pre_rows, HD), BF16),
             jax.ShapeDtypeStruct((2, dec_rows, HD), BF16),
         ),
-        in_specs=[hbm] * 12,
+        in_specs=[pl.BlockSpec(memory_space=pltpu.HBM)] * 12,
         out_specs=(vmem, vmem, vmem, vmem),
         scratch_shapes=[
             pltpu.VMEM((4, dec_rows, width), BF16),
@@ -438,6 +495,8 @@
             pltpu.SMEM(dec_lengths.shape, jnp.int32),
             pltpu.SMEM(pre_offsets.shape, jnp.int32),
             pltpu.VMEM((1, HD), F32),
+            pltpu.VMEM((rows, 2 * shard), F32),
+            pltpu.VMEM((heads * dec_rows, dec_pool.shape[1]), F32),
             dma((12,)),
             dma((3,)), dma((3,)),
             dma((CHUNKS, 4)), dma((CHUNKS, 4)),

time: 53.1 us -> 49.8 us (0.938)
  Pallas kernels: 52.4 us -> 49.1 us
    pallas_call x1, Pallas kernels: 46.4 us -> 43.1 us  [body(): pl.pallas_call(functools.partial(step_kernel, n_tok), name='attention_ste...]
where the time goes in v3:
time: 49.8 us; the launch traced here: 49.7 us
  Pallas kernels  49.1 us (99%)
  between operations  0.64 us (1%)
    pallas_call x1, Pallas kernels, body(): pl.pallas_call(functools.partial(step_kernel, n_tok), name='attention_ste...  43.1 us
    pallas_call x1, Pallas kernels, body(): pl.pallas_call(pool_kernel, name='append_rows', out_shape=(jax.ShapeDtype...  6 us

profile of v3, /device:TPU:0, one launch (start us, length us, event | category | flops | bytes accessed | tf_op | source)
XLA Modules:
  0.0 49.7 jit_solution(15681519772766155787)
XLA Ops:
  0.6 43.1 %attention_step.1 = (bf16[16,640]{1,0:T(8,128)(2,1)}, bf16[256,640]{1,0:T(8,128)(2,1)}, bf16[2,256,128]{2,1,0:T(8,128)(2,1)}, bf16[2,16,128]{2,1,0:T(8,128)(2,1)}) custom-call(bf16[16,1280]{1,0:T(8,128)(2,1)} %dec_x.1, bf16[256,1280]{1,0:T(8,128)(2,1)} %pre_x.1, bf16[5120,640]{1,0:T(8,128)(2,1)} %w_q.1, bf16[10240,128]{1,0:T(8,128)(2,1)} %bitcast.1, ...), custom_call_target="tpu_custom_call" | custom-call | tf_op jit(solution)/shard_map/attention_step/pallas_call | solution.py:465
  43.7 6.0 %append_rows.1 = (bf16[2,12288,128]{2,1,0:T(8,128)(2,1)}, bf16[16,640]{1,0:T(8,128)(2,1)}, bf16[256,640]{1,0:T(8,128)(2,1)}, bf16[2,256,128]{2,1,0:T(8,128)(2,1)}) custom-call(bf16[2,12288,128]{2,1,0:T(8,128)(2,1)} %pool.3, bf16[2,16,128]{2,1,0:T(8,128)(2,1)} %get-tuple-element.12.fresh_in, s32[16]{0:T(128)} %lengths_in.3, ...), custom_call_target="tpu_custom_call" | custom-call | tf_op jit(solution)/shard_map/append_rows/pallas_call | solution.py:517
